TPU v7x, 32 devices: a whole 2x2x4 slice. The times are simulated.
32 devices in a mesh: group: 2 (over y), expert: 4 (over z), tensor: 4 (over x, core).
Axes of the slice: x: 2, y: 2, z: 4, core: 2. Of those that a mesh axis runs over, the one named last changes fastest.
Arguments:
- tokens: bfloat16 [2048, 4096], P(('group', 'expert', 'tensor')), parts along dimension 0, may hold values from -6 to 6
- expert_ids: int32 [2048, 8], P(('group', 'expert', 'tensor')), parts along dimension 0, may hold values from 0 to 7, all different within a row; in each aligned block of 64 rows (0 to 63, 64 to 127, ...) at most 64 rows name the same one
- gate_weights: float32 [2048, 8], P(('group', 'expert', 'tensor')), parts along dimension 0, may hold values from 0.05 to 1
- w_gate: bfloat16 [16, 4096, 384], P(('expert', 'tensor')), may hold values from -0.09375 to 0.09375
- w_up: bfloat16 [16, 4096, 384], P(('expert', 'tensor')), may hold values from -0.09375 to 0.09375
- w_down: bfloat16 [16, 384, 4096], P(('expert', 'tensor')), may hold values from -0.21875 to 0.21875
Outputs:
- combined: bfloat16 [2048, 4096], P(('group', 'expert', 'tensor')), parts along dimension 0
There are 2 independent parts, one for each index of `group`. A program takes and returns all parts, laid end to end along the dimension named above; an argument that names none is the same for every part. Nothing has to cross between parts.
Inputs may be any that keep to these rules, and one draw needn't show every extreme that they name: `expert_ids`: each row names 8 different experts. Among the 64 rows of one device, no expert is named by more than 64 rows, a bound that some block reaches.
All inputs are finite; a program needn't handle non-finite values. Where the computation divides by a largest or mean magnitude, that divisor is 1e-20 or more.
Results may differ from a plain program's by a relative error of at most 0.03.
Values may be sent and summed in bfloat16 or wider, within the bound.
A program may use at most 128 MiB of HBM per device.

v0:
```python
import math

import jax
import jax.numpy as jnp
from jax import lax
from jax.experimental import pallas as pl
from jax.experimental.pallas import tpu as pltpu
from jax.sharding import PartitionSpec as P

ROT = 128


def swapped(value, axis, apart):
    mask = 2**apart
    pairs = [(source, source ^ mask) for source in range(lax.axis_size(axis))]
    return lax.ppermute(value, axis, pairs)


def hadamard():
    position = lax.iota(jnp.int32, ROT)
    common_bits = jnp.bitwise_and(position[:, None], position[None, :])
    parity = jnp.zeros((ROT, ROT), jnp.int32)
    for bit_index in range(ROT.bit_length() - 1):
        parity = parity + jnp.bitwise_and(jnp.right_shift(common_bits, bit_index), 1)
    return (1 - 2 * (parity % 2)).astype(jnp.float32) / math.sqrt(ROT)


def rotate(values, hadamard_table):
    blocks = values.reshape(values.shape[0], -1, ROT)
    turned = jnp.einsum("rbi,ij->rbj", blocks, hadamard_table, precision=lax.Precision.HIGHEST)
    return turned.reshape(values.shape)


def ring_kernel(
    tokens_ref, ids_ref, gains_ref, gate_ref, up_ref, down_ref, out_ref,
    tok, wg, wu, wd_raw, wd, mine, exch_send, exch_recv, rs_send, rs_recv, fin_send, fin_recv,
    load_sem, tok_send_sem, tok_recv_sem, pair_send_sem, pair_recv_sem,
    exch_send_sem, exch_recv_sem, rs_send_sem, rs_recv_sem, fin_sem,
):
    slots, _, rows, _ = tok.shape
    half_rows = rows // 2
    width = tokens_ref.shape[1]
    half = width // 2
    last = slots - 1

    group = lax.axis_index("group")
    along_z = lax.axis_index("expert")
    tensor = lax.axis_index("tensor")
    core = lax.rem(tensor, 2)
    along_x = tensor // 2
    length = slots // 2
    expert = along_z * 2 + along_x
    position = jnp.where(along_x == 0, along_z, slots - 1 - along_z)

    def device_at(place):
        place = lax.rem(place + slots, slots)
        x = place // length
        z = jnp.where(x == 0, place, slots - 1 - place)
        return (group, z, 2 * x + core)

    neighbours = (device_at(position + 1), device_at(position - 1))
    partner = (group, along_z, 2 * along_x + 1 - core)

    def remote(src, dst, send, recv, device):
        return pltpu.make_async_remote_copy(
            src_ref=src, dst_ref=dst, send_sem=send, recv_sem=recv,
            device_id=device, device_id_type=pl.DeviceIdType.MESH,
        )

    def tok_copy(s, way):
        part = pl.ds(way * half_rows, half_rows)
        return remote(
            tok.at[s, 0, part], tok.at[s + 1, 0, part],
            tok_send_sem.at[way, s], tok_recv_sem.at[way, s + 1], neighbours[way],
        )

    def pair_copy(s):
        return remote(tok.at[s, 0], tok.at[s, 1], pair_send_sem.at[s], pair_recv_sem.at[s], partner)

    def exch_copy(s):
        return remote(
            exch_send.at[s], exch_recv.at[s], exch_send_sem.at[s], exch_recv_sem.at[s], partner
        )

    def rs_copy(s, way):
        return remote(
            rs_send.at[s, way], rs_recv.at[s + 1, way],
            rs_send_sem.at[way, s], rs_recv_sem.at[way, s + 1], neighbours[way],
        )

    barrier = pltpu.get_barrier_semaphore()
    for device in (*neighbours, partner):
        pl.semaphore_signal(barrier, inc=1, device_id=device, device_id_type=pl.DeviceIdType.MESH)

    loads = [
        pltpu.make_async_copy(tokens_ref, tok.at[0, 0, :, pl.ds(0, width)], load_sem.at[0]),
        pltpu.make_async_copy(down_ref.at[0], wd_raw, load_sem.at[1]),
        pltpu.make_async_copy(gate_ref.at[0], wg, load_sem.at[2]),
        pltpu.make_async_copy(up_ref.at[0], wu, load_sem.at[3]),
    ]
    for load in loads:
        load.start()

    lane = lax.broadcasted_iota(jnp.int32, (rows, ROT), 1)
    lane_expert = lax.rem(lane, slots)
    lane_term = lane // slots
    weight = jnp.zeros((rows, ROT), jnp.float32)
    for k in range(ids_ref.shape[1]):
        weight = weight + jnp.where(ids_ref[:, k : k + 1] == lane_expert, gains_ref[:, k : k + 1], 0.0)
    first = weight.astype(jnp.bfloat16).astype(jnp.float32)
    second = (weight - first).astype(jnp.bfloat16).astype(jnp.float32)
    third = weight - first - second
    packed = jnp.where(
        lane_term == 0, first, jnp.where(lane_term == 1, second, jnp.where(lane_term == 2, third, 0.0))
    )
    tok[0, 0, :, width:] = packed.astype(jnp.bfloat16)

    loads[0].wait()
    pl.semaphore_wait(barrier, 3)
    tok_copy(0, 0).start()
    tok_copy(0, 1).start()
    pair_copy(0).start()

    rs_recv[0] = jnp.zeros(rs_recv.shape[1:], rs_recv.dtype)
    rs_recv[1] = jnp.zeros(rs_recv.shape[1:], rs_recv.dtype)

    bits = lax.broadcasted_iota(jnp.int32, (ROT, ROT), 0) & lax.broadcasted_iota(jnp.int32, (ROT, ROT), 1)
    bits = bits ^ (bits >> 4)
    bits = bits ^ (bits >> 2)
    bits = (bits ^ (bits >> 1)) & 1
    signs = (1 - 2 * bits).astype(jnp.float32).astype(jnp.bfloat16)
    norm = 1.0 / math.sqrt(ROT)

    loads[1].wait()
    for which in range(2):
        start = jnp.where(which == 0, core, 1 - core) * half
        for block in range(half // ROT):
            columns = pl.ds(pl.multiple_of(start + block * ROT, ROT), ROT)
            turned = jnp.dot(wd_raw[:, columns], signs, preferred_element_type=jnp.float32) * norm
            wd[which, :, block * ROT : (block + 1) * ROT] = turned.astype(jnp.bfloat16)
    loads[2].wait()
    loads[3].wait()

    def step(s, carry):
        @pl.when(s >= 1)
        def _():
            tok_copy(s - 1, 0).wait_recv()
            tok_copy(s - 1, 1).wait_recv()

            @pl.when(s < last)
            def _():
                tok_copy(s, 0).start()
                tok_copy(s, 1).start()

            pair_copy(s).start()

        pair_copy(s).wait_recv()
        x = tok[s, :, :, :width].reshape(2 * rows, width)
        gate = jnp.dot(x, wg[...], preferred_element_type=jnp.float32)
        up = jnp.dot(x, wu[...], preferred_element_type=jnp.float32)
        hidden = (gate / (1.0 + jnp.exp(-gate)) * up).astype(jnp.bfloat16)
        theirs = jnp.dot(hidden, wd[1], preferred_element_type=jnp.float32).astype(jnp.bfloat16)
        exch_send[s, :rows] = theirs[rows:]
        exch_send[s, rows:] = theirs[:rows]
        exch_copy(s).start()
        mine[...] = jnp.dot(hidden, wd[0], preferred_element_type=jnp.float32)
        tail = tok[s, :, :, width:].reshape(2 * rows, ROT).astype(jnp.float32)
        wide = lax.broadcasted_iota(jnp.int32, (2 * rows, ROT), 1)
        gain = jnp.sum(jnp.where(lax.rem(wide, slots) == expert, tail, 0.0), axis=1, keepdims=True)
        exch_copy(s).wait_recv()

        @pl.when(s >= 2)
        def _():
            rs_copy(s - 1, 0).wait_recv()
            rs_copy(s - 1, 1).wait_recv()

        for block in range(half // ROT):
            columns = slice(block * ROT, (block + 1) * ROT)
            value = mine[:, columns] + exch_recv[s, :, columns].astype(jnp.float32)
            scale = jnp.max(jnp.abs(value), axis=1, keepdims=True) + 1e-06
            quantized = (value * (1.0 / scale) + 3.0).astype(jnp.bfloat16)
            restored = (quantized.astype(jnp.float32) - 3.0) * (scale * gain)
            for way in range(2):
                for which in range(2):
                    top = which * rows + way * half_rows
                    total = restored[top : top + half_rows] + rs_recv[s, way, which, :, columns].astype(
                        jnp.float32
                    )
                    rs_send[s, way, which, :, columns] = total.astype(jnp.bfloat16)

        @pl.when(s >= 1)
        def _():
            rs_copy(s, 0).start()
            rs_copy(s, 1).start()

        return carry

    lax.fori_loop(0, slots, step, 0)

    rs_copy(last, 0).wait_recv()
    rs_copy(last, 1).wait_recv()
    doubled = jnp.concatenate([signs, signs], axis=0)
    for which in (1, 0):
        for block in range(half // ROT):
            columns = slice(block * ROT, (block + 1) * ROT)
            pieces = [
                rs_send[0, way, which, :, columns].astype(jnp.float32)
                + rs_recv[slots, way, which, :, columns].astype(jnp.float32)
                for way in range(2)
            ]
            total = jnp.concatenate(pieces, axis=0)
            high = total.astype(jnp.bfloat16)
            low = (total - high.astype(jnp.float32)).astype(jnp.bfloat16)
            turned = jnp.dot(
                jnp.concatenate([high, low], axis=1), doubled, preferred_element_type=jnp.float32
            )
            result = (turned * norm).astype(jnp.bfloat16)
            if which == 1:
                fin_send[:, columns] = result
            else:
                out_ref[:, pl.ds(pl.multiple_of(core * half + block * ROT, ROT), ROT)] = result
        if which == 1:
            fin_copy = remote(fin_send, fin_recv, fin_sem.at[0], fin_sem.at[1], partner)
            fin_copy.start()

    def drain(s, carry):
        pair_copy(s).wait_send()
        exch_copy(s).wait_send()
        for way in range(2):
            @pl.when(s < last)
            def _():
                tok_copy(s, way).wait_send()

            @pl.when(s >= 1)
            def _():
                rs_copy(s, way).wait_send()
        return carry

    lax.fori_loop(0, slots, drain, 0)
    fin_copy.wait_recv()
    out_ref[:, pl.ds(pl.multiple_of((1 - core) * half, half), half)] = fin_recv[...]
    fin_copy.wait_send()


def ring_layer(tokens, expert_ids, gate_weights, w_gate, w_up, w_down):
    rows, width = tokens.shape
    hidden = w_gate.shape[2]
    half = width // 2
    slots = 2 * lax.axis_size("expert")
    dma, bf16 = pltpu.SemaphoreType.DMA, jnp.bfloat16
    anywhere = pl.BlockSpec(memory_space=pl.ANY)
    vmem = pl.BlockSpec(memory_space=pltpu.VMEM)
    return pl.pallas_call(
        ring_kernel,
        out_shape=jax.ShapeDtypeStruct((rows, width), bf16),
        in_specs=[anywhere, vmem, vmem, anywhere, anywhere, anywhere],
        out_specs=vmem,
        scratch_shapes=[
            pltpu.VMEM((slots, 2, rows, width + ROT), bf16),
            pltpu.VMEM((width, hidden), bf16),
            pltpu.VMEM((width, hidden), bf16),
            pltpu.VMEM((hidden, width), bf16),
            pltpu.VMEM((2, hidden, half), bf16),
            pltpu.VMEM((2 * rows, half), jnp.float32),
            pltpu.VMEM((slots, 2 * rows, half), bf16),
            pltpu.VMEM((slots, 2 * rows, half), bf16),
            pltpu.VMEM((slots, 2, 2, rows // 2, half), bf16),
            pltpu.VMEM((slots + 1, 2, 2, rows // 2, half), bf16),
            pltpu.VMEM((rows, half), bf16),
            pltpu.VMEM((rows, half), bf16),
            dma((4,)),
            dma((2, slots)),
            dma((2, slots)),
            dma((slots,)),
            dma((slots,)),
            dma((slots,)),
            dma((slots,)),
            dma((2, slots)),
            dma((2, slots + 1)),
            dma((2,)),
        ],
        compiler_params=pltpu.CompilerParams(
            collective_id=0, has_side_effects=True, vmem_limit_bytes=56 * 1024 * 1024
        ),
    )(tokens, expert_ids, gate_weights, w_gate, w_up, w_down)


def local(tokens, expert_ids, gate_weights, w_gate, w_up, w_down):
    hadamard_table = hadamard()
    tok_rows, model_width = tokens.shape
    top_count = expert_ids.shape[1]
    n_expert = lax.axis_size("expert")
    n_tensor = lax.axis_size("tensor")
    devices = n_expert * n_tensor
    experts = devices // 2
    capacity = max(2, min(tok_rows, 5 * tok_rows * top_count // (4 * experts)))
    if capacity == tok_rows and n_tensor == 4 and experts == 2 * n_expert and experts * 3 <= ROT:
        return ring_layer(tokens, expert_ids, gate_weights, w_gate, w_up, w_down)
    half_width = model_width // 2
    my_half = lax.axis_index("tensor") % 2
    gate_mat = w_gate[0]
    up_mat = w_up[0]
    down_mat = w_down[0]
    flat_ids = expert_ids.reshape(-1)
    onehot = (flat_ids[:, None] == lax.iota(jnp.int32, experts)[None, :]).astype(jnp.int32)
    slot_index = jnp.sum((jnp.cumsum(onehot, axis=0, dtype=jnp.int32) - onehot) * onehot, axis=1)
    lower_row = 2 * flat_ids * capacity + slot_index
    upper_row = lower_row + capacity
    copies = tokens[lax.iota(jnp.int32, tok_rows * top_count) // top_count]
    both_rows = jnp.concatenate([lower_row, upper_row])
    outgoing = jnp.zeros((devices * capacity, model_width), jnp.bfloat16)
    outgoing = outgoing.at[both_rows].set(jnp.concatenate([copies, copies], axis=0))
    received = lax.all_to_all(
        outgoing.reshape(devices, capacity, model_width),
        ("expert", "tensor"),
        split_axis=0,
        concat_axis=0,
        tiled=True,
    )
    token_rows = received.reshape(-1, model_width)
    item_count = received.shape[1]
    gate_proj = jnp.dot(token_rows, gate_mat, preferred_element_type=jnp.float32)
    up_proj = jnp.dot(token_rows, up_mat, preferred_element_type=jnp.float32)
    hidden = (jax.nn.silu(gate_proj) * up_proj).astype(jnp.bfloat16)
    partial_out = jnp.dot(hidden, down_mat, preferred_element_type=jnp.float32)
    own_part = lax.dynamic_slice_in_dim(partial_out, my_half * half_width, half_width, 1)
    other_part = lax.dynamic_slice_in_dim(partial_out, (1 - my_half) * half_width, half_width, 1)
    partner_part = swapped(other_part.astype(jnp.bfloat16), "tensor", 0).astype(other_part.dtype)
    summed = own_part + partner_part
    rotated = rotate(summed, hadamard_table).reshape(-1, half_width // ROT, ROT)
    scales = jnp.max(jnp.abs(rotated), axis=-1) + 1e-06
    quantized = (rotated / scales[:, :, None] + 3.0).astype(jnp.bfloat16)
    quant_out = quantized.reshape(devices, item_count, half_width)
    scale_out = scales.reshape(devices, item_count, half_width // ROT)
    back_quant, back_scales = (
        lax.all_to_all(quant_out, ("expert", "tensor"), split_axis=0, concat_axis=0, tiled=True),
        lax.all_to_all(
            scale_out.astype(jnp.bfloat16),
            ("expert", "tensor"),
            split_axis=0,
            concat_axis=0,
            tiled=True,
        ).astype(scale_out.dtype),
    )
    flat_quant = back_quant.reshape(devices * capacity, half_width // ROT, ROT)
    flat_scales = back_scales.reshape(devices * capacity, half_width // ROT)

    def restore(row_index):
        picked = (flat_quant[row_index].astype(jnp.float32) - 3.0) * flat_scales[row_index][
            :, :, None
        ]
        return picked.reshape(-1, half_width)

    restored = jnp.concatenate([restore(lower_row), restore(upper_row)], axis=1)
    mixed = jnp.einsum(
        "tkd,tk->td",
        restored.reshape(tok_rows, top_count, model_width),
        gate_weights,
        precision=lax.Precision.HIGHEST,
    )
    return rotate(mixed, hadamard_table).astype(jnp.bfloat16)


def solution(mesh):
    in_specs = (
        P(("group", "expert", "tensor"), None),
        P(("group", "expert", "tensor"), None),
        P(("group", "expert", "tensor"), None),
        P(("expert", "tensor"), None, None),
        P(("expert", "tensor"), None, None),
        P(("expert", "tensor"), None, None),
    )
    out_specs = P(("group", "expert", "tensor"), None)
    return jax.shard_map(local, mesh=mesh, in_specs=in_specs, out_specs=out_specs, check_vma=False)
```

profile of v0, /device:TPU:0, one launch (start us, length us, event | category | flops | bytes accessed | tf_op | source)
XLA Modules:
  0.0 97.7 jit_solution(7388150776813790550)
XLA Ops:
  0.0 1.4 %copy.7.ids_ref = s32[64,8]{1,0:T(8,128)} copy(s32[64,8]{0,1:T(8,128)} %param.7) | data formatting | bytes 4096 | tf_op args[1]
  1.4 1.4 %copy.8.gains_ref = f32[64,8]{1,0:T(8,128)} copy(f32[64,8]{0,1:T(8,128)} %param.8) | data formatting | bytes 4096 | tf_op args[2]
  2.8 93.1 %shard_map.64 = bf16[64,4096]{1,0:T(8,128)(2,1)} custom-call(bf16[64,4096]{1,0:T(8,128)(2,1)} %tokens_ref.1, s32[64,8]{1,0:T(8,128)} %copy.7.ids_ref, f32[64,8]{1,0:T(8,128)} %copy.8.gains_ref, bf16[1,4096,384]{2,1,0:T(8,128)(2,1)} %gate_ref.1, bf16[1,4096,384]{2,1,0:T(8,128)(2,1)} %up_ref.1, bf16[1,384,4096]{2,1,0:T(8,128)(2,1)} %down_ref.1), custom_call_target="tpu_custom_call" | custom-call | tf_op jit(solution)/shard_map/pallas_call | solution.py:253
  95.8 1.9 %copy.10 = bf16[64,4096]{1,0:T(8,128)(2,1)} copy(bf16[64,4096]{1,0:T(8,128)(2,1)} %shard_map.64) | data formatting | bytes 1048576
where the time goes:
time: 98 us; the launch traced here: 97.7 us
  Pallas kernels  93.1 us (95%)
  local copies, waits for them, and re-layouts  4.62 us (5%)
    pallas_call x1, Pallas kernels, ring_layer(): pl.pallas_call(ring_kernel, out_shape=jax.ShapeDtypeStruct((rows, width),...  93.1 us
    unnamed x3, local copies, waits for them, and re-layouts  4.62 us

commit v1 on v0

--- a/solution.py
+++ b/solution.py
@@ -31,10 +31,13 @@
     return turned.reshape(values.shape)
 
 
+PIECES = 2
+
+
 def ring_kernel(
     tokens_ref, ids_ref, gains_ref, gate_ref, up_ref, down_ref, out_ref,
     tok, wg, wu, wd_raw, wd, mine, exch_send, exch_recv, rs_send, rs_recv, fin_send, fin_recv,
-    load_sem, tok_send_sem, tok_recv_sem, pair_send_sem, pair_recv_sem,
+    ids, gains, load_sem, tok_send_sem, tok_recv_sem, pair_send_sem, pair_recv_sem,
     exch_send_sem, exch_recv_sem, rs_send_sem, rs_recv_sem, fin_sem,
 ):
     slots, _, rows, _ = tok.shape
@@ -42,6 +45,7 @@
     width = tokens_ref.shape[1]
     half = width // 2
     last = slots - 1
+    pieces, part = rs_send.shape[2], rs_send.shape[5]
 
     group = lax.axis_index("group")
     along_z = lax.axis_index("expert")
@@ -68,9 +72,9 @@
         )
 
     def tok_copy(s, way):
-        part = pl.ds(way * half_rows, half_rows)
+        mine_way = pl.ds(way * half_rows, half_rows)
         return remote(
-            tok.at[s, 0, part], tok.at[s + 1, 0, part],
+            tok.at[s, 0, mine_way], tok.at[s + 1, 0, mine_way],
             tok_send_sem.at[way, s], tok_recv_sem.at[way, s + 1], neighbours[way],
         )
 
@@ -82,10 +86,15 @@
             exch_send.at[s], exch_recv.at[s], exch_send_sem.at[s], exch_recv_sem.at[s], partner
         )
 
-    def rs_copy(s, way):
+    def rs_copy(s, way, piece):
         return remote(
-            rs_send.at[s, way], rs_recv.at[s + 1, way],
-            rs_send_sem.at[way, s], rs_recv_sem.at[way, s + 1], neighbours[way],
+            rs_send.at[s, way, piece], rs_recv.at[s + 1, way, piece],
+            rs_send_sem.at[way, piece, s], rs_recv_sem.at[way, piece, s + 1], neighbours[way],
+        )
+
+    def fin_copy(piece):
+        return remote(
+            fin_send.at[piece], fin_recv.at[piece], fin_sem.at[0, piece], fin_sem.at[1, piece], partner
         )
 
     barrier = pltpu.get_barrier_semaphore()
@@ -97,25 +106,32 @@
         pltpu.make_async_copy(down_ref.at[0], wd_raw, load_sem.at[1]),
         pltpu.make_async_copy(gate_ref.at[0], wg, load_sem.at[2]),
         pltpu.make_async_copy(up_ref.at[0], wu, load_sem.at[3]),
+        pltpu.make_async_copy(ids_ref, ids, load_sem.at[4]),
+        pltpu.make_async_copy(gains_ref, gains, load_sem.at[5]),
     ]
+    loads = loads[4:] + loads[:4]
     for load in loads:
         load.start()
 
-    lane = lax.broadcasted_iota(jnp.int32, (rows, ROT), 1)
-    lane_expert = lax.rem(lane, slots)
-    lane_term = lane // slots
-    weight = jnp.zeros((rows, ROT), jnp.float32)
-    for k in range(ids_ref.shape[1]):
-        weight = weight + jnp.where(ids_ref[:, k : k + 1] == lane_expert, gains_ref[:, k : k + 1], 0.0)
+    loads[0].wait()
+    loads[1].wait()
+    place = lax.broadcasted_iota(jnp.int32, (ROT, rows), 0)
+    place_expert = lax.rem(place, slots)
+    place_term = place // slots
+    weight = jnp.zeros((ROT, rows), jnp.float32)
+    for k in range(ids.shape[0]):
+        weight = weight + jnp.where(ids[k : k + 1, :] == place_expert, gains[k : k + 1, :], 0.0)
     first = weight.astype(jnp.bfloat16).astype(jnp.float32)
     second = (weight - first).astype(jnp.bfloat16).astype(jnp.float32)
     third = weight - first - second
     packed = jnp.where(
-        lane_term == 0, first, jnp.where(lane_term == 1, second, jnp.where(lane_term == 2, third, 0.0))
-    )
-    tok[0, 0, :, width:] = packed.astype(jnp.bfloat16)
-
-    loads[0].wait()
+        place_term == 0,
+        first,
+        jnp.where(place_term == 1, second, jnp.where(place_term == 2, third, 0.0)),
+    )
+    tok[0, 0, :, width:] = packed.T.astype(jnp.bfloat16)
+
+    loads[2].wait()
     pl.semaphore_wait(barrier, 3)
     tok_copy(0, 0).start()
     tok_copy(0, 1).start()
@@ -131,34 +147,35 @@
     signs = (1 - 2 * bits).astype(jnp.float32).astype(jnp.bfloat16)
     norm = 1.0 / math.sqrt(ROT)
 
-    loads[1].wait()
+    loads[3].wait()
     for which in range(2):
         start = jnp.where(which == 0, core, 1 - core) * half
         for block in range(half // ROT):
             columns = pl.ds(pl.multiple_of(start + block * ROT, ROT), ROT)
             turned = jnp.dot(wd_raw[:, columns], signs, preferred_element_type=jnp.float32) * norm
             wd[which, :, block * ROT : (block + 1) * ROT] = turned.astype(jnp.bfloat16)
-    loads[2].wait()
-    loads[3].wait()
+    loads[4].wait()
+    loads[5].wait()
 
     def step(s, carry):
-        @pl.when(s >= 1)
-        def _():
-            tok_copy(s - 1, 0).wait_recv()
-            tok_copy(s - 1, 1).wait_recv()
-
-            @pl.when(s < last)
-            def _():
-                tok_copy(s, 0).start()
-                tok_copy(s, 1).start()
-
-            pair_copy(s).start()
-
         pair_copy(s).wait_recv()
         x = tok[s, :, :, :width].reshape(2 * rows, width)
         gate = jnp.dot(x, wg[...], preferred_element_type=jnp.float32)
         up = jnp.dot(x, wu[...], preferred_element_type=jnp.float32)
         hidden = (gate / (1.0 + jnp.exp(-gate)) * up).astype(jnp.bfloat16)
+
+        @pl.when(s < last)
+        def _():
+            tok_copy(s, 0).wait_recv()
+            tok_copy(s, 1).wait_recv()
+
+            @pl.when(s + 1 < last)
+            def _():
+                tok_copy(s + 1, 0).start()
+                tok_copy(s + 1, 1).start()
+
+            pair_copy(s + 1).start()
+
         theirs = jnp.dot(hidden, wd[1], preferred_element_type=jnp.float32).astype(jnp.bfloat16)
         exch_send[s, :rows] = theirs[rows:]
         exch_send[s, rows:] = theirs[:rows]
@@ -169,59 +186,59 @@
         gain = jnp.sum(jnp.where(lax.rem(wide, slots) == expert, tail, 0.0), axis=1, keepdims=True)
         exch_copy(s).wait_recv()
 
-        @pl.when(s >= 2)
-        def _():
-            rs_copy(s - 1, 0).wait_recv()
-            rs_copy(s - 1, 1).wait_recv()
-
         for block in range(half // ROT):
             columns = slice(block * ROT, (block + 1) * ROT)
             value = mine[:, columns] + exch_recv[s, :, columns].astype(jnp.float32)
             scale = jnp.max(jnp.abs(value), axis=1, keepdims=True) + 1e-06
             quantized = (value * (1.0 / scale) + 3.0).astype(jnp.bfloat16)
-            restored = (quantized.astype(jnp.float32) - 3.0) * (scale * gain)
+            mine[:, columns] = (quantized.astype(jnp.float32) - 3.0) * (scale * gain)
+
+        for piece in range(pieces):
             for way in range(2):
+                @pl.when(s >= 2)
+                def _():
+                    rs_copy(s - 1, way, piece).wait_recv()
+
                 for which in range(2):
                     top = which * rows + way * half_rows
-                    total = restored[top : top + half_rows] + rs_recv[s, way, which, :, columns].astype(
-                        jnp.float32
-                    )
-                    rs_send[s, way, which, :, columns] = total.astype(jnp.bfloat16)
-
-        @pl.when(s >= 1)
-        def _():
-            rs_copy(s, 0).start()
-            rs_copy(s, 1).start()
+                    total = mine[top : top + half_rows, piece * part : (piece + 1) * part]
+                    total = total + rs_recv[s, way, piece, which].astype(jnp.float32)
+                    rs_send[s, way, piece, which] = total.astype(jnp.bfloat16)
+
+                @pl.when(s >= 1)
+                def _():
+                    rs_copy(s, way, piece).start()
 
         return carry
 
     lax.fori_loop(0, slots, step, 0)
 
-    rs_copy(last, 0).wait_recv()
-    rs_copy(last, 1).wait_recv()
     doubled = jnp.concatenate([signs, signs], axis=0)
-    for which in (1, 0):
-        for block in range(half // ROT):
-            columns = slice(block * ROT, (block + 1) * ROT)
-            pieces = [
-                rs_send[0, way, which, :, columns].astype(jnp.float32)
-                + rs_recv[slots, way, which, :, columns].astype(jnp.float32)
-                for way in range(2)
-            ]
-            total = jnp.concatenate(pieces, axis=0)
-            high = total.astype(jnp.bfloat16)
-            low = (total - high.astype(jnp.float32)).astype(jnp.bfloat16)
-            turned = jnp.dot(
-                jnp.concatenate([high, low], axis=1), doubled, preferred_element_type=jnp.float32
-            )
-            result = (turned * norm).astype(jnp.bfloat16)
+    for piece in range(pieces):
+        for way in range(2):
+            rs_copy(last, way, piece).wait_recv()
+        for which in (1, 0):
+            for block in range(part // ROT):
+                inner = slice(block * ROT, (block + 1) * ROT)
+                start = piece * part + block * ROT
+                sums = [
+                    rs_send[0, way, piece, which, :, inner].astype(jnp.float32)
+                    + rs_recv[slots, way, piece, which, :, inner].astype(jnp.float32)
+                    for way in range(2)
+                ]
+                total = jnp.concatenate(sums, axis=0)
+                high = total.astype(jnp.bfloat16)
+                low = (total - high.astype(jnp.float32)).astype(jnp.bfloat16)
+                turned = jnp.dot(
+                    jnp.concatenate([high, low], axis=1), doubled, preferred_element_type=jnp.float32
+                )
+                result = (turned * norm).astype(jnp.bfloat16)
+                if which == 1:
+                    fin_send[piece, :, inner] = result
+                else:
+                    out_ref[:, pl.ds(pl.multiple_of(core * half + start, ROT), ROT)] = result
             if which == 1:
-                fin_send[:, columns] = result
-            else:
-                out_ref[:, pl.ds(pl.multiple_of(core * half + block * ROT, ROT), ROT)] = result
-        if which == 1:
-            fin_copy = remote(fin_send, fin_recv, fin_sem.at[0], fin_sem.at[1], partner)
-            fin_copy.start()
+                fin_copy(piece).start()
 
     def drain(s, carry):
         pair_copy(s).wait_send()
@@ -233,13 +250,16 @@
 
             @pl.when(s >= 1)
             def _():
-                rs_copy(s, way).wait_send()
+                for piece in range(pieces):
+                    rs_copy(s, way, piece).wait_send()
         return carry
 
     lax.fori_loop(0, slots, drain, 0)
-    fin_copy.wait_recv()
-    out_ref[:, pl.ds(pl.multiple_of((1 - core) * half, half), half)] = fin_recv[...]
-    fin_copy.wait_send()
+    for piece in range(pieces):
+        fin_copy(piece).wait_recv()
+        start = (1 - core) * half + piece * part
+        out_ref[:, pl.ds(pl.multiple_of(start, part), part)] = fin_recv[piece]
+        fin_copy(piece).wait_send()
 
 
 def ring_layer(tokens, expert_ids, gate_weights, w_gate, w_up, w_down):
@@ -247,13 +267,14 @@
     hidden = w_gate.shape[2]
     half = width // 2
     slots = 2 * lax.axis_size("expert")
+    pieces = PIECES
     dma, bf16 = pltpu.SemaphoreType.DMA, jnp.bfloat16
     anywhere = pl.BlockSpec(memory_space=pl.ANY)
     vmem = pl.BlockSpec(memory_space=pltpu.VMEM)
     return pl.pallas_call(
         ring_kernel,
         out_shape=jax.ShapeDtypeStruct((rows, width), bf16),
-        in_specs=[anywhere, vmem, vmem, anywhere, anywhere, anywhere],
+        in_specs=[anywhere] * 6,
         out_specs=vmem,
         scratch_shapes=[
             pltpu.VMEM((slots, 2, rows, width + ROT), bf16),
@@ -264,25 +285,27 @@
             pltpu.VMEM((2 * rows, half), jnp.float32),
             pltpu.VMEM((slots, 2 * rows, half), bf16),
             pltpu.VMEM((slots, 2 * rows, half), bf16),
-            pltpu.VMEM((slots, 2, 2, rows // 2, half), bf16),
-            pltpu.VMEM((slots + 1, 2, 2, rows // 2, half), bf16),
-            pltpu.VMEM((rows, half), bf16),
-            pltpu.VMEM((rows, half), bf16),
-            dma((4,)),
+            pltpu.VMEM((slots, 2, pieces, 2, rows // 2, half // pieces), bf16),
+            pltpu.VMEM((slots + 1, 2, pieces, 2, rows // 2, half // pieces), bf16),
+            pltpu.VMEM((pieces, rows, half // pieces), bf16),
+            pltpu.VMEM((pieces, rows, half // pieces), bf16),
+            pltpu.VMEM((expert_ids.shape[1], rows), jnp.int32),
+            pltpu.VMEM((expert_ids.shape[1], rows), jnp.float32),
+            dma((6,)),
             dma((2, slots)),
             dma((2, slots)),
             dma((slots,)),
             dma((slots,)),
             dma((slots,)),
             dma((slots,)),
-            dma((2, slots)),
-            dma((2, slots + 1)),
-            dma((2,)),
+            dma((2, pieces, slots)),
+            dma((2, pieces, slots + 1)),
+            dma((2, pieces)),
         ],
         compiler_params=pltpu.CompilerParams(
             collective_id=0, has_side_effects=True, vmem_limit_bytes=56 * 1024 * 1024
         ),
-    )(tokens, expert_ids, gate_weights, w_gate, w_up, w_down)
+    )(tokens, expert_ids.T, gate_weights.T, w_gate, w_up, w_down)
 
 
 def local(tokens, expert_ids, gate_weights, w_gate, w_up, w_down):

time: 98 us -> 93.6 us (0.955)
  local copies, waits for them, and re-layouts: 4.62 us -> 1.87 us
  Pallas kernels: 93.1 us -> 91.5 us
    unnamed x3 -> x1, local copies, waits for them, and re-layouts: 4.62 us -> 1.87 us
    pallas_call x1, Pallas kernels: 93.1 us -> 91.5 us  [ring_layer(): pl.pallas_call(ring_kernel, out_shape=jax.ShapeDtypeStruct((rows, width),...]
where the time goes in v1:
time: 93.6 us; the launch traced here: 93.4 us
  Pallas kernels  91.5 us (98%)
  local copies, waits for them, and re-layouts  1.87 us (2%)
    pallas_call x1, Pallas kernels, ring_layer(): pl.pallas_call(ring_kernel, out_shape=jax.ShapeDtypeStruct((rows, width),...  91.5 us

profile of v1, /device:TPU:0, one launch (start us, length us, event | category | flops | bytes accessed | tf_op | source)
XLA Modules:
  0.0 93.4 jit_solution(12916592732501328863)
XLA Ops:
  0.0 91.5 %shard_map.64 = bf16[64,4096]{1,0:T(8,128)(2,1)} custom-call(bf16[64,4096]{1,0:T(8,128)(2,1)} %tokens_ref.1, s32[8,64]{1,0:T(8,128)} %bitcast.2, f32[8,64]{1,0:T(8,128)} %bitcast.3, bf16[1,4096,384]{2,1,0:T(8,128)(2,1)} %gate_ref.1, bf16[1,4096,384]{2,1,0:T(8,128)(2,1)} %up_ref.1, bf16[1,384,4096]{2,1,0:T(8,128)(2,1)} %down_ref.1), custom_call_target="tpu_custom_call" | custom-call | tf_op jit(solution)/shard_map/pallas_call | solution.py:274
  91.6 1.9 %copy.8 = bf16[64,4096]{1,0:T(8,128)(2,1)} copy(bf16[64,4096]{1,0:T(8,128)(2,1)} %shard_map.64) | data formatting | bytes 1048576

commit v2 on v1

--- a/solution.py
+++ b/solution.py
@@ -31,20 +31,22 @@
     return turned.reshape(values.shape)
 
 
-PIECES = 2
+PIECES = 4
 
 
 def ring_kernel(
     tokens_ref, ids_ref, gains_ref, gate_ref, up_ref, down_ref, out_ref,
-    tok, wg, wu, wd_raw, wd, mine, exch_send, exch_recv, rs_send, rs_recv, fin_send, fin_recv,
-    ids, gains, load_sem, tok_send_sem, tok_recv_sem, pair_send_sem, pair_recv_sem,
+    tok, wg, wu, wd_raw, wd, mine, exch_send, exch_recv, rs_send, rs_recv, fin_send, fin_own,
+    ids, gains, wt, load_sem, tok_send_sem, tok_recv_sem, pair_send_sem, pair_recv_sem,
     exch_send_sem, exch_recv_sem, rs_send_sem, rs_recv_sem, fin_sem,
+    wt_send_sem, wt_recv_sem, wt_pair_send_sem, wt_pair_recv_sem,
 ):
     slots, _, rows, _ = tok.shape
     half_rows = rows // 2
     width = tokens_ref.shape[1]
     half = width // 2
     last = slots - 1
+    hops = wt.shape[1] - 1
     pieces, part = rs_send.shape[2], rs_send.shape[5]
 
     group = lax.axis_index("group")
@@ -71,15 +73,16 @@
             device_id=device, device_id_type=pl.DeviceIdType.MESH,
         )
 
-    def tok_copy(s, way):
+    def tok_copy(s, way, src=None):
         mine_way = pl.ds(way * half_rows, half_rows)
         return remote(
-            tok.at[s, 0, mine_way], tok.at[s + 1, 0, mine_way],
+            tok.at[s, 0, mine_way] if src is None else src.at[mine_way], tok.at[s + 1, 0, mine_way],
             tok_send_sem.at[way, s], tok_recv_sem.at[way, s + 1], neighbours[way],
         )
 
-    def pair_copy(s):
-        return remote(tok.at[s, 0], tok.at[s, 1], pair_send_sem.at[s], pair_recv_sem.at[s], partner)
+    def pair_copy(s, src=None):
+        src = tok.at[s, 0] if src is None else src
+        return remote(src, tok.at[s, 1], pair_send_sem.at[s], pair_recv_sem.at[s], partner)
 
     def exch_copy(s):
         return remote(
@@ -92,17 +95,36 @@
             rs_send_sem.at[way, piece, s], rs_recv_sem.at[way, piece, s + 1], neighbours[way],
         )
 
+    def wt_copy(s, way):
+        return remote(
+            wt.at[way, s, 0], wt.at[way, s + 1, 0],
+            wt_send_sem.at[way, s], wt_recv_sem.at[way, s + 1], neighbours[way],
+        )
+
+    def wt_pair(s, way):
+        return remote(
+            wt.at[way, s, 0], wt.at[way, s, 1],
+            wt_pair_send_sem.at[way, s], wt_pair_recv_sem.at[way, s], partner,
+        )
+
+    def fin_place(piece):
+        start = core * half + piece * part
+        return out_ref.at[:, pl.ds(pl.multiple_of(start, ROT), part)]
+
     def fin_copy(piece):
         return remote(
-            fin_send.at[piece], fin_recv.at[piece], fin_sem.at[0, piece], fin_sem.at[1, piece], partner
-        )
+            fin_send.at[piece], fin_place(piece), fin_sem.at[0, piece], fin_sem.at[1, piece], partner
+        )
+
+    def keep_copy(piece):
+        return pltpu.make_async_copy(fin_own.at[piece], fin_place(piece), fin_sem.at[2, piece])
 
     barrier = pltpu.get_barrier_semaphore()
     for device in (*neighbours, partner):
         pl.semaphore_signal(barrier, inc=1, device_id=device, device_id_type=pl.DeviceIdType.MESH)
 
     loads = [
-        pltpu.make_async_copy(tokens_ref, tok.at[0, 0, :, pl.ds(0, width)], load_sem.at[0]),
+        pltpu.make_async_copy(tokens_ref, tok.at[0, 0], load_sem.at[0]),
         pltpu.make_async_copy(down_ref.at[0], wd_raw, load_sem.at[1]),
         pltpu.make_async_copy(gate_ref.at[0], wg, load_sem.at[2]),
         pltpu.make_async_copy(up_ref.at[0], wu, load_sem.at[3]),
@@ -113,29 +135,23 @@
     for load in loads:
         load.start()
 
+    pl.semaphore_wait(barrier, 3)
+    tok_copy(0, 0, tokens_ref).start()
+    tok_copy(0, 1, tokens_ref).start()
+    pair_copy(0, tokens_ref).start()
+
     loads[0].wait()
     loads[1].wait()
-    place = lax.broadcasted_iota(jnp.int32, (ROT, rows), 0)
-    place_expert = lax.rem(place, slots)
-    place_term = place // slots
-    weight = jnp.zeros((ROT, rows), jnp.float32)
+    named = lax.broadcasted_iota(jnp.int32, (slots, rows), 0)
+    weight = jnp.zeros((slots, rows), jnp.float32)
     for k in range(ids.shape[0]):
-        weight = weight + jnp.where(ids[k : k + 1, :] == place_expert, gains[k : k + 1, :], 0.0)
-    first = weight.astype(jnp.bfloat16).astype(jnp.float32)
-    second = (weight - first).astype(jnp.bfloat16).astype(jnp.float32)
-    third = weight - first - second
-    packed = jnp.where(
-        place_term == 0,
-        first,
-        jnp.where(place_term == 1, second, jnp.where(place_term == 2, third, 0.0)),
-    )
-    tok[0, 0, :, width:] = packed.T.astype(jnp.bfloat16)
-
-    loads[2].wait()
-    pl.semaphore_wait(barrier, 3)
-    tok_copy(0, 0).start()
-    tok_copy(0, 1).start()
-    pair_copy(0).start()
+        weight = weight + jnp.where(ids[k : k + 1, :] == named, gains[k : k + 1, :], 0.0)
+    weight = jnp.concatenate([weight, weight], axis=1)
+    for way in range(2):
+        wt[way, 0, 0] = weight
+    for way in range(2):
+        wt_copy(0, way).start()
+        wt_pair(0, way).start()
 
     rs_recv[0] = jnp.zeros(rs_recv.shape[1:], rs_recv.dtype)
     rs_recv[1] = jnp.zeros(rs_recv.shape[1:], rs_recv.dtype)
@@ -154,36 +170,64 @@
             columns = pl.ds(pl.multiple_of(start + block * ROT, ROT), ROT)
             turned = jnp.dot(wd_raw[:, columns], signs, preferred_element_type=jnp.float32) * norm
             wd[which, :, block * ROT : (block + 1) * ROT] = turned.astype(jnp.bfloat16)
+    loads[2].wait()
     loads[4].wait()
     loads[5].wait()
 
     def step(s, carry):
         pair_copy(s).wait_recv()
-        x = tok[s, :, :, :width].reshape(2 * rows, width)
+        x = tok[s].reshape(2 * rows, width)
         gate = jnp.dot(x, wg[...], preferred_element_type=jnp.float32)
         up = jnp.dot(x, wu[...], preferred_element_type=jnp.float32)
         hidden = (gate / (1.0 + jnp.exp(-gate)) * up).astype(jnp.bfloat16)
 
         @pl.when(s < last)
         def _():
-            tok_copy(s, 0).wait_recv()
-            tok_copy(s, 1).wait_recv()
-
-            @pl.when(s + 1 < last)
-            def _():
-                tok_copy(s + 1, 0).start()
-                tok_copy(s + 1, 1).start()
+            for way in range(2):
+                tok_copy(s, way).wait_recv()
+
+                @pl.when(s + 1 < last)
+                def _():
+                    tok_copy(s + 1, way).start()
 
             pair_copy(s + 1).start()
+
+        @pl.when(s < hops)
+        def _():
+            for way in range(2):
+                wt_copy(s, way).wait_recv()
+
+                @pl.when(s + 1 < hops)
+                def _():
+                    wt_copy(s + 1, way).start()
+
+                wt_pair(s + 1, way).start()
 
         theirs = jnp.dot(hidden, wd[1], preferred_element_type=jnp.float32).astype(jnp.bfloat16)
         exch_send[s, :rows] = theirs[rows:]
         exch_send[s, rows:] = theirs[:rows]
         exch_copy(s).start()
         mine[...] = jnp.dot(hidden, wd[0], preferred_element_type=jnp.float32)
-        tail = tok[s, :, :, width:].reshape(2 * rows, ROT).astype(jnp.float32)
-        wide = lax.broadcasted_iota(jnp.int32, (2 * rows, ROT), 1)
-        gain = jnp.sum(jnp.where(lax.rem(wide, slots) == expert, tail, 0.0), axis=1, keepdims=True)
+
+        @pl.when(s <= hops)
+        def _():
+            for way in range(2):
+                wt_pair(s, way).wait_recv()
+
+        near = s <= hops
+        apart = jnp.where(near, s, slots - s)
+        behind = jnp.where(near, 0, 1)
+        lane = lax.broadcasted_iota(jnp.int32, (slots, 2 * rows), 1)
+        backward = lax.rem(lane, rows) >= half_rows
+        own = jnp.where(backward, wt[1 - behind, apart, 0], wt[behind, apart, 0])
+        other = jnp.where(backward, wt[1 - behind, apart, 1], wt[behind, apart, 1])
+        row = lax.broadcasted_iota(jnp.int32, (slots, 2 * rows), 0)
+        chosen = jnp.where(row == expert, jnp.where(lane < rows, own, other), 0.0)
+        chosen = jnp.sum(chosen, axis=0, keepdims=True)
+        diagonal = lax.broadcasted_iota(jnp.int32, (2 * rows, 2 * rows), 0) == lax.broadcasted_iota(
+            jnp.int32, (2 * rows, 2 * rows), 1
+        )
+        gain = jnp.sum(jnp.where(diagonal, chosen, 0.0), axis=1, keepdims=True)
         exch_copy(s).wait_recv()
 
         for block in range(half // ROT):
@@ -220,7 +264,6 @@
         for which in (1, 0):
             for block in range(part // ROT):
                 inner = slice(block * ROT, (block + 1) * ROT)
-                start = piece * part + block * ROT
                 sums = [
                     rs_send[0, way, piece, which, :, inner].astype(jnp.float32)
                     + rs_recv[slots, way, piece, which, :, inner].astype(jnp.float32)
@@ -236,14 +279,24 @@
                 if which == 1:
                     fin_send[piece, :, inner] = result
                 else:
-                    out_ref[:, pl.ds(pl.multiple_of(core * half + start, ROT), ROT)] = result
+                    fin_own[piece, :, inner] = result
             if which == 1:
                 fin_copy(piece).start()
+            else:
+                keep_copy(piece).start()
 
     def drain(s, carry):
         pair_copy(s).wait_send()
         exch_copy(s).wait_send()
         for way in range(2):
+            @pl.when(s < hops)
+            def _():
+                wt_copy(s, way).wait_send()
+
+            @pl.when(s <= hops)
+            def _():
+                wt_pair(s, way).wait_send()
+
             @pl.when(s < last)
             def _():
                 tok_copy(s, way).wait_send()
@@ -257,8 +310,7 @@
     lax.fori_loop(0, slots, drain, 0)
     for piece in range(pieces):
         fin_copy(piece).wait_recv()
-        start = (1 - core) * half + piece * part
-        out_ref[:, pl.ds(pl.multiple_of(start, part), part)] = fin_recv[piece]
+        keep_copy(piece).wait()
         fin_copy(piece).wait_send()
 
 
@@ -267,17 +319,16 @@
     hidden = w_gate.shape[2]
     half = width // 2
     slots = 2 * lax.axis_size("expert")
-    pieces = PIECES
+    pieces, hops = PIECES, slots // 2
     dma, bf16 = pltpu.SemaphoreType.DMA, jnp.bfloat16
     anywhere = pl.BlockSpec(memory_space=pl.ANY)
-    vmem = pl.BlockSpec(memory_space=pltpu.VMEM)
     return pl.pallas_call(
         ring_kernel,
         out_shape=jax.ShapeDtypeStruct((rows, width), bf16),
         in_specs=[anywhere] * 6,
-        out_specs=vmem,
+        out_specs=anywhere,
         scratch_shapes=[
-            pltpu.VMEM((slots, 2, rows, width + ROT), bf16),
+            pltpu.VMEM((slots, 2, rows, width), bf16),
             pltpu.VMEM((width, hidden), bf16),
             pltpu.VMEM((width, hidden), bf16),
             pltpu.VMEM((hidden, width), bf16),
@@ -291,6 +342,7 @@
             pltpu.VMEM((pieces, rows, half // pieces), bf16),
             pltpu.VMEM((expert_ids.shape[1], rows), jnp.int32),
             pltpu.VMEM((expert_ids.shape[1], rows), jnp.float32),
+            pltpu.VMEM((2, hops + 1, 2, slots, 2 * rows), jnp.float32),
             dma((6,)),
             dma((2, slots)),
             dma((2, slots)),
@@ -300,7 +352,11 @@
             dma((slots,)),
             dma((2, pieces, slots)),
             dma((2, pieces, slots + 1)),
-            dma((2, pieces)),
+            dma((3, pieces)),
+            dma((2, hops + 1)),
+            dma((2, hops + 1)),
+            dma((2, hops + 1)),
+            dma((2, hops + 1)),
         ],
         compiler_params=pltpu.CompilerParams(
             collective_id=0, has_side_effects=True, vmem_limit_bytes=56 * 1024 * 1024
@@ -317,7 +373,7 @@
     devices = n_expert * n_tensor
     experts = devices // 2
     capacity = max(2, min(tok_rows, 5 * tok_rows * top_count // (4 * experts)))
-    if capacity == tok_rows and n_tensor == 4 and experts == 2 * n_expert and experts * 3 <= ROT:
+    if capacity == tok_rows and n_tensor == 4 and experts == 2 * n_expert and 2 * tok_rows == ROT:
         return ring_layer(tokens, expert_ids, gate_weights, w_gate, w_up, w_down)
     half_width = model_width // 2
     my_half = lax.axis_index("tensor") % 2

time: 93.6 us -> 91.9 us (0.982)
  Pallas kernels: 91.5 us -> 89.9 us
    pallas_call x1, Pallas kernels: 91.5 us -> 89.9 us  [ring_layer(): pl.pallas_call(ring_kernel, out_shape=jax.ShapeDtypeStruct((rows, width),...]
where the time goes in v2:
time: 91.9 us; the launch traced here: 91.8 us
  Pallas kernels  89.9 us (98%)
  local copies, waits for them, and re-layouts  1.87 us (2%)
    pallas_call x1, Pallas kernels, ring_layer(): pl.pallas_call(ring_kernel, out_shape=jax.ShapeDtypeStruct((rows, width),...  89.9 us
    unnamed x1, local copies, waits for them, and re-layouts  1.87 us

profile of v2, /device:TPU:0, one launch (start us, length us, event | category | flops | bytes accessed | tf_op | source)
XLA Modules:
  0.0 91.8 jit_solution(7877910207519103504)
XLA Ops:
  0.0 89.9 %shard_map.64 = bf16[64,4096]{1,0:T(8,128)(2,1)} custom-call(bf16[64,4096]{1,0:T(8,128)(2,1)} %tokens_ref.1, s32[8,64]{1,0:T(8,128)} %bitcast.2, f32[8,64]{1,0:T(8,128)} %bitcast.3, bf16[1,4096,384]{2,1,0:T(8,128)(2,1)} %gate_ref.1, bf16[1,4096,384]{2,1,0:T(8,128)(2,1)} %up_ref.1, bf16[1,384,4096]{2,1,0:T(8,128)(2,1)} %down_ref.1), custom_call_target="tpu_custom_call" | custom-call | tf_op jit(solution)/shard_map/pallas_call | solution.py:325
  89.9 1.9 %copy.8 = bf16[64,4096]{1,0:T(8,128)(2,1)} copy(bf16[64,4096]{1,0:T(8,128)(2,1)} %shard_map.64) | data formatting | bytes 1048576

commit v3 on v2

--- a/solution.py
+++ b/solution.py
@@ -230,14 +230,14 @@
         gain = jnp.sum(jnp.where(diagonal, chosen, 0.0), axis=1, keepdims=True)
         exch_copy(s).wait_recv()
 
-        for block in range(half // ROT):
-            columns = slice(block * ROT, (block + 1) * ROT)
-            value = mine[:, columns] + exch_recv[s, :, columns].astype(jnp.float32)
-            scale = jnp.max(jnp.abs(value), axis=1, keepdims=True) + 1e-06
-            quantized = (value * (1.0 / scale) + 3.0).astype(jnp.bfloat16)
-            mine[:, columns] = (quantized.astype(jnp.float32) - 3.0) * (scale * gain)
-
         for piece in range(pieces):
+            for block in range(piece * part // ROT, (piece + 1) * part // ROT):
+                columns = slice(block * ROT, (block + 1) * ROT)
+                value = mine[:, columns] + exch_recv[s, :, columns].astype(jnp.float32)
+                scale = jnp.max(jnp.abs(value), axis=1, keepdims=True) + 1e-06
+                quantized = (value * (1.0 / scale) + 3.0).astype(jnp.bfloat16)
+                mine[:, columns] = (quantized.astype(jnp.float32) - 3.0) * (scale * gain)
+
             for way in range(2):
                 @pl.when(s >= 2)
                 def _():

time: 91.9 us -> 91.8 us (level)
  no operation moved by 1% of the time
where the time goes in v3:
time: 91.8 us; the launch traced here: 91.7 us
  Pallas kernels  89.8 us (98%)
  local copies, waits for them, and re-layouts  1.87 us (2%)
    pallas_call x1, Pallas kernels, ring_layer(): pl.pallas_call(ring_kernel, out_shape=jax.ShapeDtypeStruct((rows, width),...  89.8 us
    unnamed x1, local copies, waits for them, and re-layouts  1.87 us

profile of v3, /device:TPU:0, one launch (start us, length us, event | category | flops | bytes accessed | tf_op | source)
XLA Modules:
  0.0 91.7 jit_solution(12323872746407853776)
XLA Ops:
  0.0 89.8 %shard_map.64 = bf16[64,4096]{1,0:T(8,128)(2,1)} custom-call(bf16[64,4096]{1,0:T(8,128)(2,1)} %tokens_ref.1, s32[8,64]{1,0:T(8,128)} %bitcast.2, f32[8,64]{1,0:T(8,128)} %bitcast.3, bf16[1,4096,384]{2,1,0:T(8,128)(2,1)} %gate_ref.1, bf16[1,4096,384]{2,1,0:T(8,128)(2,1)} %up_ref.1, bf16[1,384,4096]{2,1,0:T(8,128)(2,1)} %down_ref.1), custom_call_target="tpu_custom_call" | custom-call | tf_op jit(solution)/shard_map/pallas_call | solution.py:325
  89.8 1.9 %copy.8 = bf16[64,4096]{1,0:T(8,128)(2,1)} copy(bf16[64,4096]{1,0:T(8,128)(2,1)} %shard_map.64) | data formatting | bytes 1048576
